TPU v7x, 32 devices: a whole 2x2x4 slice. The times are simulated.
32 devices in a mesh: dp: 16 (over z, x, core), tensor: 2 (over y).
Axes of the slice: x: 2, y: 2, z: 4, core: 2. Of those that a mesh axis runs over, the one named last changes fastest.
Arguments:
- patches: bfloat16 [16384, 768], P('dp'), may hold values from -6 to 6
- image_ids: int32 [16, 1024], P('dp'), may hold values from 0 to 7, never falling along the last dimension, each value on 1 to 256 neighbouring positions
- valid: int32 [16, 1024], P('dp'), may hold values 0 or 1
- mask_pos: int32 [16, 1024], P('dp'), may hold values 0 or 1
- mask_token: bfloat16 [768], replicated, may hold values from -5 to 5
- ln1_gain: bfloat16 [768], replicated, may hold values from 0.5 to 1.5
- ln1_bias: bfloat16 [768], replicated, may hold values from -1.5 to 1.5
- w_qkv: bfloat16 [768, 3, 768], P(None, None, 'tensor'), may hold values from -0.21875 to 0.21875
- b_qv: bfloat16 [2, 768], P(None, 'tensor'), may hold values from -2.5 to 2.5
- w_proj: bfloat16 [768, 768], P('tensor'), may hold values from -0.875 to 0.875
- b_proj: bfloat16 [768], replicated, may hold values from -1.5 to 1.5
- ln2_gain: bfloat16 [768], replicated, may hold values from 0.5 to 1.5
- ln2_bias: bfloat16 [768], replicated, may hold values from -1.5 to 1.5
- w_up: bfloat16 [768, 3072], P('dp', 'tensor'), may hold values from -0.21875 to 0.21875
- b_up: bfloat16 [3072], P('tensor'), may hold values from -2.5 to 2.5
- w_down: bfloat16 [3072, 768], P('tensor', 'dp'), may hold values from -0.109375 to 0.109375
- b_down: bfloat16 [768], replicated, may hold values from -1.5 to 1.5
- cotangent: bfloat16 [16384, 768], P('dp'), may hold values from -6 to 6
Outputs:
- mixed: bfloat16 [16384, 768], P('dp')
- grad_input: float32 [16384, 768], P('dp')
- grad_mask_token: float32 [768], replicated
- grad_ln1_gain: float32 [768], replicated
- grad_ln1_bias: float32 [768], replicated
- grad_w_qkv: float32 [768, 3, 768], P(None, None, 'tensor')
- grad_b_qv: float32 [2, 768], P(None, 'tensor')
- grad_w_proj: float32 [768, 768], P('tensor')
- grad_b_proj: float32 [768], replicated
- grad_ln2_gain: float32 [768], replicated
- grad_ln2_bias: float32 [768], replicated
- grad_w_up: float32 [768, 3072], P('dp', 'tensor')
- grad_b_up: float32 [3072], P('tensor')
- grad_w_down: float32 [3072, 768], P('tensor', 'dp')
- grad_b_down: float32 [768], replicated
Inputs may be any that keep to these rules, and one draw needn't show every extreme that they name: `image_ids`: within each pack the ids never fall along the patches; an image has 1 to 256 patches and one of each pack has exactly 256.
All inputs are finite; a program needn't handle non-finite values. No bound on the sum of `valid` or of `mask_pos` on one device may be relied on, other than what follows from the above.
Results may differ from a plain program's by a relative error of at most 0.013.
Values may be sent and summed in bfloat16 or wider, within the bound.
A program may use at most 192 MiB of HBM per device.

v0:
```python
from functools import partial

import jax
import jax.numpy as jnp
from jax import lax
from jax.experimental import pallas as pl
from jax.experimental.pallas import tpu as pltpu
from jax.sharding import PartitionSpec as P

BF = jnp.bfloat16
F32 = jnp.float32
MESH = pl.DeviceIdType.MESH
EPS = 1e-06
T = 1024
H = 512
D = 768
HL = 384
BLK = 256
WIN = 768
CUT = 640
SENT, LANDED, LOCAL = 148, 143, 17


def nn(a, b):
    return lax.dot_general(a, b, (((1,), (0,)), ((), ())), preferred_element_type=F32)


def nt(a, b):
    return lax.dot_general(a, b, (((1,), (1,)), ((), ())), preferred_element_type=F32)


def tn(a, b):
    return lax.dot_general(a, b, (((0,), (0,)), ((), ())), preferred_element_type=F32)


def rowsum(v):
    return jnp.sum(v, axis=0, keepdims=True)


def lane_half(shape):
    return lax.broadcasted_iota(jnp.int32, shape, 1) < 64


def stats(v):
    mean = jnp.sum(v, axis=-1, keepdims=True) * (1.0 / D)
    cent = v - mean
    var = jnp.sum(cent * cent, axis=-1, keepdims=True) * (1.0 / D)
    return cent, lax.rsqrt(var + EPS)


def norm_back(xhat, r, d, gain):
    e = d * gain
    m1 = jnp.sum(e, axis=-1, keepdims=True) * (1.0 / D)
    m2 = jnp.sum(e * xhat, axis=-1, keepdims=True) * (1.0 / D)
    return r * (e - m1 - xhat * m2)


def mega(
    patches, ids, live, hidden_pos, token_b, ln1g_b, ln1b_b, bproj_b, ln2g_b, ln2b_b, bdown_b, wqkv_h, bqv_b, wproj,
    up, dn, bup, cot,
    mixed, gin, fA, gup, gdn, vout,
    n1, nT, qkv, attO, attF, wpf, Wu, Wd, mid, n2, dml, dmlT, outA, dn2A, rO, rN, act, dh, gU, gD,
    rG, rX, sy, ry, sc, rc, dO, rgp, rA, lseT, bupA, vecA, vR, pat, wqkv, codec, coder, vec, mixS, ginS, fS,
    gS, ssem, rsem, lsem,
):
    d = lax.axis_index("dp")
    t = lax.axis_index("tensor")
    z = lax.div(d, 4)
    x = lax.rem(lax.div(d, 2), 2)
    c = lax.rem(d, 2)
    zk = (z, z + 1 - 2 * lax.rem(z, 2), lax.rem(z + 2, 4), 3 - z)
    xr = (x, 1 - x)
    tr = (t, 1 - t)

    def dev(zz, xx, cc, tt):
        return ((zz * 2 + xx) * 2 + cc, tt)

    core = dev(z, x, 1 - c, t)
    xp = dev(z, 1 - x, c, t)
    yp = dev(z, x, c, 1 - t)
    z1 = dev(zk[1], x, c, t)
    z2 = dev(zk[2], x, c, t)
    z3 = dev(zk[3], x, c, t)
    mid_z = (z == 1) | (z == 2)
    end_z = (z == 0) | (z == 3)

    pending = []
    flushed = set()
    slots = [0]

    def slot():
        slots[0] += 1
        return slots[0] - 1

    def xchg(src, dst, to, when=None, land=None):
        i = len(pending)
        cp = pltpu.make_async_remote_copy(
            src_ref=src, dst_ref=dst, send_sem=ssem.at[i], recv_sem=rsem.at[slot() if land is None else land],
            device_id=to, device_id_type=MESH,
        )
        pending.append((cp, when))
        if when is None:
            cp.start()
        else:
            pl.when(when)(cp.start)
        return cp

    def landed(dst, land, frm):
        pltpu.make_async_remote_copy(
            src_ref=dst, dst_ref=dst, send_sem=ssem.at[0], recv_sem=rsem.at[land], device_id=frm, device_id_type=MESH
        ).wait_recv()

    def flush(cps):
        cps = set(id(cp) for cp in cps)
        for cp, when in pending:
            if id(cp) in cps and id(cp) not in flushed:
                flushed.add(id(cp))
                if when is None:
                    cp.wait_send()
                else:
                    pl.when(when)(cp.wait_send)

    def al(v, m):
        return pl.multiple_of(v, m)

    bar = pltpu.get_barrier_semaphore()
    peers = (core, xp, yp, z1, z2, z3)
    for p in peers:
        pl.semaphore_signal(bar, inc=1, device_id=p, device_id_type=MESH)
    loads = []

    def load(src, dst):
        cp = pltpu.make_async_copy(src, dst, lsem.at[len(loads)])
        cp.start()
        loads.append(cp)
        return cp

    lpat = load(patches, pat)
    lwq = load(wqkv_h, wqkv)
    code = ids[...] + 16 * live[...] + 32 * hidden_pos[...]
    coder[...] = code
    codec[...] = jnp.broadcast_to(code.astype(F32), (128, T)).T.astype(jnp.int32)
    for i, row in enumerate((token_b, ln1g_b, ln1b_b, bproj_b, ln2g_b, ln2b_b, bdown_b)):
        vec[i : i + 1, :] = row[...].astype(F32).reshape(1, D)
    bqv = bqv_b[...].astype(F32)
    bupA[0] = jnp.zeros((8, D), F32)
    for i in range(2):
        bupA[0, i : i + 1, :] = bup[i * D : i * D + D].astype(F32).reshape(1, D)
    pl.semaphore_wait(bar, len(peers))

    own = al(t * H, H)
    oth = al((1 - t) * H, H)
    cslot = al(c * H, H)
    sslot = al((1 - c) * H, H)
    W = (Wu, Wd)
    shards = (up, dn)

    def wblk(a, k, xx, yy):
        return W[a].at[tr[yy], pl.ds(al((zk[k] * 2 + xr[xx]) * 96, 32), 96), :]

    ccp = []
    mine = al((z * 2 + x) * 96 + c * 48, 16)
    for a in (0, 1):
        ccp.append(
            xchg(shards[a].at[:, pl.ds(al((1 - c) * D, 128), D)], W[a].at[t, pl.ds(mine, 48), :], core)
        )
    whalf = pl.ds(al(c * 192, 64), 192)
    cwp = xchg(wproj.at[whalf, :], wpf.at[t, whalf, :], yp)
    cbup = xchg(bupA.at[0, pl.ds(c, 1), :], bupA.at[1, pl.ds(c, 1), :], yp)
    cdml = xchg(cot.at[pl.ds(own, H), :], dml.at[pl.ds(cslot, H), :], core)
    ldml = load(cot.at[pl.ds(own, H), :], dml.at[pl.ds(cslot, H), :])
    lwp = load(wproj, wpf.at[t])
    for a in (0, 1):
        W[a][t, pl.ds(mine, 48), :] = shards[a][:, pl.ds(al(c * D, 128), D)]

    zc, xc, yc = {}, {}, {}

    chains = {
        "u": lambda k: wblk(0, k, 0, 0),
        "d": lambda k: wblk(1, k, 0, 0),
        "e": lambda k: wblk(1, k, 0, 1),
        "b": lambda k: Wu.at[tr[1], pl.ds(al(zk[k] * 192, 64), 192), CUT:D],
    }

    def zsend(q, k):
        zc[(q, k)] = xchg(chains[q](0), chains[q](0), z1 if k == 1 else z2)

    def zstart(q):
        zsend(q, 1)
        zsend(q, 2)

    def zstep(q):
        zc[(q, 2)].wait_recv()
        zc[(q, 3)] = xchg(chains[q](2), chains[q](2), z1)

    def zend(q):
        zc[(q, 3)].wait_recv()

    def xsend(a, k, yy):
        xc[(a, k, yy)] = xchg(wblk(a, k, 0, yy), wblk(a, k, 0, yy), xp)

    def ysend(a, k, xx):
        ref = wblk(a, k, xx, 0)
        if a == 0:
            ref = W[0].at[t, pl.ds(al((zk[k] * 2 + xr[xx]) * 96, 32), 96), 0:CUT]
        yc[(a, k, xx)] = xchg(ref, ref, yp)

    def bown(tt):
        return W[0].at[tt, pl.ds(al((z * 2 + x) * 96, 32), 96), CUT:D]

    token = vec[0:1, :]
    ln1g = vec[1:2, :]
    ln1b = vec[2:3, :]

    def start_rows(r0):
        m = lax.shift_right_logical(codec[pl.ds(r0, BLK), 0:1], 5) == 1
        return m, jnp.where(m, token, pat[pl.ds(r0, BLK), :].astype(F32))

    def ln1_block(b, carry):
        r0 = al(b * BLK, BLK)
        _, v = start_rows(r0)
        cent, r = stats(v)
        nb = (cent * r * ln1g + ln1b).astype(BF)
        n1[pl.ds(r0, BLK), :] = nb
        for s in range(3):
            y = nn(nb, wqkv[s])
            if s == 0:
                y = y + bqv[0:1, :]
            if s == 2:
                y = y + bqv[1:2, :]
            qkv[s, pl.ds(r0, BLK), :] = y.astype(BF)
        return carry

    lpat.wait()
    lwq.wait()
    lax.fori_loop(0, 1, ln1_block, 0)
    for a in (0, 1):
        ccp[a].wait_recv()
    zstart("u")
    zsend("d", 1)
    xsend(0, 0, 0)
    xsend(1, 0, 0)
    lax.fori_loop(1, 4, ln1_block, 0)

    def masked_pair(block, scale=None):
        low = lane_half(block.shape)
        zero = jnp.zeros_like(block)
        if scale is not None:
            block = block * jnp.asarray(scale, BF)
        return jnp.where(low, block, zero), jnp.where(low, zero, block)

    def att_block(half, edge):
        qb = half * 3 if edge else 1 + half
        win = H if edge else WIN
        r0 = al(qb * BLK, BLK)
        ws = al(half * H if edge else half * BLK, BLK)
        cr = codec[pl.ds(r0, BLK), 0:1]
        cw = coder[:, pl.ds(ws, win)]
        rid = r0 + lax.broadcasted_iota(jnp.int32, (BLK, win), 0)
        cid = ws + lax.broadcasted_iota(jnp.int32, (BLK, win), 1)
        ok = ((cr & 15) == (cw & 15)) & (((cw & 16) == 16) | (rid == cid))
        dn2A[0:BLK, 0:win] = jnp.where(ok, 0.0, -1e30)
        lane = lax.broadcasted_iota(jnp.int32, (BLK, 128), 1)

        def pair(p, lacc):
            cols = pl.ds(al(p * 128, 128), 128)
            qs = masked_pair(qkv[0, pl.ds(r0, BLK), cols], 0.125)
            kp = qkv[1, pl.ds(ws, win), cols]
            vp = qkv[2, pl.ds(ws, win), cols]
            outs = []
            for h in range(2):
                s = nt(qs[h], kp) + dn2A[0:BLK, 0:win]
                top = jnp.max(s, axis=-1, keepdims=True)
                e = jnp.exp(s - top)
                l = jnp.sum(e, axis=-1, keepdims=True)
                o = nn(e.astype(BF), vp) * (1.0 / l)
                outs.append(o)
                lacc = jnp.where(lane == (2 * p + h), top + jnp.log(l), lacc)
            attO[pl.ds(r0, BLK), cols] = jnp.where(lane_half((BLK, 128)), outs[0], outs[1]).astype(BF)
            return lacc

        lacc = lax.fori_loop(0, 3, pair, jnp.zeros((BLK, 128), F32))
        lseT[:, pl.ds(r0, BLK)] = lacc.T[0:8, :]
        return r0

    catt = []

    def att_send(r0):
        catt.append(xchg(attO.at[pl.ds(r0, BLK), :], attF.at[t, pl.ds(al(r0 - oth, BLK), BLK), :], yp))

    att_send(att_block(1 - t, True))
    att_send(att_block(1 - t, False))
    ysend(1, 0, 0)
    yb = xchg(bown(t), bown(t), yp)
    zc[("u", 1)].wait_recv()
    xsend(0, 1, 0)
    zstep("u")
    zsend("d", 2)
    xsend(0, 2, 0)
    cwp.wait_recv()
    cwc = xchg(wpf.at[1 - t, whalf, :], wpf.at[1 - t, whalf, :], core)
    for k in range(3):
        ysend(0, k, 0)
    att_block(t, True)
    att_block(t, False)
    attF[t] = attO[pl.ds(own, H), :]
    zend("u")
    xsend(0, 3, 0)
    zc[("d", 1)].wait_recv()
    xsend(1, 1, 0)
    ysend(0, 3, 0)

    bproj = vec[3:4, :]
    ln2g = vec[4:5, :]
    ln2b = vec[5:6, :]
    bdown = vec[6:7, :]
    ldml.wait()
    lwp.wait()
    for cp in catt:
        cp.wait_recv()
    cwc.wait_recv()

    def mid_block(b, carry):
        o0 = al(b * BLK, BLK)
        _, v = start_rows(al(own + o0, BLK))
        m = v + (nn(attF[0, pl.ds(o0, BLK), :], wpf[0]) + nn(attF[1, pl.ds(o0, BLK), :], wpf[1])) + bproj
        mid[pl.ds(o0, BLK), :] = m
        cent, r = stats(m)
        n2[pl.ds(al(cslot + o0, BLK), BLK), :] = (cent * r * ln2g + ln2b).astype(BF)
        return carry

    lax.fori_loop(0, 2, mid_block, 0)
    cn2 = xchg(n2.at[pl.ds(cslot, H), :], n2.at[pl.ds(cslot, H), :], core)
    zstep("d")
    xsend(1, 2, 0)
    yc[(1, 0, 0)].wait_recv()
    zstart("e")
    yb.wait_recv()
    xb = xchg(bown(1 - t), bown(1 - t), xp)
    cdml.wait_recv()
    cn2.wait_recv()
    nT[...] = n2[...].T
    dmlT[...] = dml[...].T
    cbup.wait_recv()
    for k in range(4):
        xc[(0, k, 0)].wait_recv()
        ysend(0, k, 1)
    zend("d")
    xsend(1, 3, 0)
    xsend(1, 0, 1)

    G = (gU, gD)
    rs = {}

    def addto(dst, src):
        dst[...] = (dst[...].astype(F32) + src[...].astype(F32)).astype(BF)

    def rs_x(a, j):
        rs[(a, j)] = [xchg(G[a].at[j, 1, h * 2 : h * 2 + 2], rG.at[a, j, h * 2 : h * 2 + 2], xp) for h in (0, 1)]

    rland = {(r, q): slot() for r in ((0, 0, 0), (0, 0, 1), (0, 1, 0), (1, 0, 0), (1, 1, 0)) for q in range(4, 9)}

    def rslot(r, q):
        a, j, xx = r
        if xx == 0:
            return rG.at[a, j, q]
        return rX.at[0] if q == 8 else rG.at[a, j, q - 4]

    def gblk(r, k):
        a, j, xx = r
        return G[a].at[j, xx, zk[k]]

    def rpass(r, k, to, q, when):
        xchg(gblk(r, k), rslot(r, q), to, when, rland[(r, q)])

    def radd(r, k, q):
        landed(rslot(r, q), rland[(r, q)], z1)
        addto(gblk(r, k), rslot(r, q))

    def rs_z0(r):
        for k, q in ((3, 4), (2, 5), (1, 6)):
            rpass(r, k, z1, q, end_z)

    def rs_z1(a, j):
        for cp in rs[(a, j)]:
            cp.wait_recv()
        for zz in range(4):
            addto(G[a].at[j, 0, zz], rG.at[a, j, zz])
        rs_z0((a, j, 0))

    def rs_z2(r):
        pl.when(mid_z)(partial(radd, r, 2, 4))
        rpass(r, 2, z3, 7, mid_z)
        pl.when(mid_z)(partial(radd, r, 3, 5))
        rpass(r, 3, z3, 8, mid_z)

    def rs_z3(r):
        pl.when(mid_z)(partial(radd, r, 1, 7))
        rpass(r, 1, z1, 8, mid_z)

    def rs_zsum(r):
        pl.when(mid_z)(partial(radd, r, 0, 6))
        radd(r, 0, 8)

    def rs_xlast():
        rs_zsum((0, 0, 1))
        rs["xlast"] = xchg(gblk((0, 0, 1), 0), rX.at[1], xp)

    def rs_sum(a, j):
        rs_zsum((a, j, 0))
        total = gblk((a, j, 0), 0)[...].astype(F32)
        if (a, j) == (0, 0):
            rs["xlast"].wait_recv()
            total = total + rX[1].astype(F32)
        return total

    def rs_y(a):
        sy[a] = rs_sum(a, 1).astype(BF)
        rs[(a, "y")] = xchg(sy.at[a], ry.at[a], yp)

    def rs_c(a):
        total = rs_sum(a, 0)
        rs[(a, "y")].wait_recv()
        sc[a] = total + ry[a].astype(F32)
        rs[(a, "c")] = xchg(sc.at[a, pl.ds(al((1 - c) * 48, 16), 48), :], rc.at[a], core)

    def rs_end(a):
        gS[a, :, pl.ds(al(c * D, 128), D)] = sc[a, pl.ds(al(c * 48, 16), 48), :]
        rs[(a, "c")].wait_recv()
        gS[a, :, pl.ds(al((1 - c) * D, 128), D)] = rc[a]
        load(gS.at[a], (gup, gdn)[a])

    bsums = []

    def ff_act(j):
        yy = tr[j]
        bu = bupA[j, pl.ds(c, 1), :]

        def block(b, carry):
            rows = pl.ds(al(b * BLK, BLK), BLK)
            hid = nn(n2[rows, :], Wu[yy]) + bu
            phi = 0.5 * (1.0 + lax.erf(hid * 0.7071067811865476))
            a = (hid * phi).astype(BF)
            act[rows, :] = a
            dh[rows, :] = (phi + hid * (jnp.exp(hid * hid * -0.5) * 0.3989422804014327)).astype(BF)
            return carry

        lax.fori_loop(0, 4, block, 0)

    def ff_out(j):
        yy = tr[j]

        def block(b, carry):
            rows = pl.ds(al(b * BLK, BLK), BLK)
            o = nt(act[rows, :], Wd[yy])
            if j == 0:
                outA[rows, :] = o
            else:
                outA[rows, :] += o
            return carry

        lax.fori_loop(0, 4, block, 0)

    def ff_bwd(j):
        yy = tr[j]

        def block(b, carry):
            rows = pl.ds(al(b * BLK, BLK), BLK)
            dhid = (nn(dml[rows, :], Wd[yy]) * dh[rows, :].astype(F32)).astype(BF)
            dh[rows, :] = dhid
            g = nt(dhid, Wu[yy])
            if j == 0:
                dn2A[rows, :] = g
            else:
                dn2A[rows, :] += g
            return carry + rowsum(dhid.astype(F32))

        bsums.append(lax.fori_loop(0, 4, block, jnp.zeros((1, D), F32)))

    def ff_grads(j, left, right, out):
        def gw_block(b, carry):
            r = nn(left[pl.ds(al(b * 192, 64), 192), :], right[...]).astype(BF)
            for xa in range(2):
                out[j, lax.rem(xa + x, 2), b] = r[xa * 96 : xa * 96 + 96]
            return carry

        lax.fori_loop(0, 4, gw_block, 0)

    def ff_gu(j):
        ff_grads(j, nT, dh, gU)

    def ff_gd(j):
        ff_grads(j, dmlT, act, gD)

    zrow = jnp.zeros((1, D), F32)
    ff_act(0)
    xb.wait_recv()
    zstart("b")
    ff_gd(0)
    zc[("e", 1)].wait_recv()
    xsend(1, 1, 1)
    for k in range(4):
        xc[(1, k, 0)].wait_recv()
    ff_out(0)
    zstep("e")
    xsend(1, 2, 1)
    ff_bwd(0)
    zstep("b")
    zend("e")
    xsend(1, 3, 1)
    rs_x(1, 0)
    ff_gu(0)
    rs_z0((0, 0, 1))
    rs_z0((0, 0, 0))
    zc[("b", 1)].wait_recv()
    zend("b")
    for k in range(4):
        yc[(0, k, 0)].wait_recv()
        yc[(0, k, 1)].wait_recv()
    ff_act(1)
    ff_gd(1)
    rs_x(1, 1)
    for k in range(4):
        xc[(1, k, 1)].wait_recv()
    ff_bwd(1)

    flush([cn2])
    n2[0:H, :] = dn2A[pl.ds(sslot, H), :].astype(BF)
    cN = xchg(n2.at[0:H, :], rN, core)
    ff_out(1)
    n2[H:T, :] = outA[pl.ds(sslot, H), :].astype(BF)
    cO = xchg(n2.at[H:T, :], rO, core)
    rs_z2((0, 0, 1))
    ff_gu(1)
    rs_x(0, 1)
    flush(catt)
    cN.wait_recv()
    flush([cN])

    sums = [zrow, zrow, zrow, zrow]
    cda = []
    for o in (t, 1 - t):
        o0 = al(o * BLK, BLK)
        rows = pl.ds(o0, BLK)
        crow = pl.ds(al(cslot + o0, BLK), BLK)
        dnb = dn2A[crow, :] + rN[rows, :].astype(F32)
        cent, r = stats(mid[rows, :])
        xhat = cent * r
        ct = dml[crow, :].astype(F32)
        dm = ct + norm_back(xhat, r, dnb, ln2g)
        db = dm.astype(BF)
        n2[rows, :] = db
        attO[rows, :] = nt(db, wpf[1 - t]).astype(BF)
        orow = pl.ds(al(own + o0, BLK), BLK)
        cda.append(xchg(attO.at[rows, :], dO.at[orow, :], yp))
        dO[orow, :] = nt(db, wpf[t]).astype(BF)
        dn2A[crow, :] = dm
        for i, term in enumerate((dnb * xhat, dnb, db.astype(F32), ct)):
            sums[i] = sums[i] + rowsum(term)
    s2g, s2b, sp, sd = sums

    cO.wait_recv()
    cmix = []

    def mixed_block(o):
        o0 = al(o * BLK, BLK)
        rows = pl.ds(o0, BLK)
        crow = pl.ds(al(cslot + o0, BLK), BLK)
        out = mid[rows, :] + (outA[crow, :] + rO[rows, :].astype(F32)) + bdown
        mixS[rows, :] = out.astype(BF)
        mid[rows, :] = dn2A[crow, :]

    def mixed_send(i):
        orow = pl.ds(own + i * 128, 128)
        rows = slice(i * 128, i * 128 + 128)
        cmix.append(xchg(mixS.at[rows, :], mixed.at[orow, :], yp))
        load(mixS.at[rows, :], mixed.at[orow, :])

    mixed_block(0)
    mixed_block(1)
    mixed_send(0)
    mixed_send(1)
    mixed_send(2)
    rs_z3((0, 0, 1))
    rs_z2((0, 0, 0))
    outA[...] = jnp.zeros((T, D), F32)
    nT[...] = n1[...].T
    rs_z1(1, 0)

    def att_back(half, edge):
        qb = half * 3 if edge else 1 + half
        wl = H if edge else WIN
        r0 = al(qb * BLK, BLK)
        ws = al(half * H if edge else half * BLK, BLK)
        cw = codec[pl.ds(ws, wl), 0:1]
        cr = coder[:, pl.ds(r0, BLK)]
        rid = r0 + lax.broadcasted_iota(jnp.int32, (wl, BLK), 1)
        cid = ws + lax.broadcasted_iota(jnp.int32, (wl, BLK), 0)
        ok = ((cr & 15) == (cw & 15)) & (((cw & 16) == 16) | (rid == cid))
        dn2A[0:wl, 0:BLK] = jnp.where(ok, 0.0, -1e30)
        rows = pl.ds(r0, BLK)
        win = pl.ds(ws, wl)

        def pair(p, carry):
            cols = pl.ds(al(p * 128, 128), 128)
            vcols = pl.ds(al(HL + p * 128, 128), 128)
            qp = qkv[0, rows, cols]
            op = dO[rows, cols]
            qs = masked_pair(qp, 0.125)
            os = masked_pair(op)
            kp = qkv[1, win, cols]
            vp = qkv[2, win, cols]
            dqs, dks, dvs = [], [], []
            for h in range(2):
                lse = lseT[pl.ds(2 * p + h, 1), rows]
                pr = jnp.exp(nt(kp, qs[h]) + dn2A[0:wl, 0:BLK] - lse)
                dp = nt(vp, os[h])
                inner = rowsum(pr * dp)
                ds = (pr * (dp - inner)).astype(BF)
                dvs.append(nn(pr.astype(BF), op))
                dks.append(nn(ds, qp))
                dqs.append(tn(ds, kp))
            low = lane_half((BLK, 128))
            lowk = lane_half((wl, 128))
            act[rows, cols] = (jnp.where(low, dqs[0], dqs[1]) * 0.125).astype(BF)
            outA[win, cols] += jnp.where(lowk, dks[0], dks[1])
            outA[win, vcols] += jnp.where(lowk, dvs[0], dvs[1])
            return carry

        lax.fori_loop(0, 3, pair, 0)

    def finish_rows(r0):
        rows = pl.ds(r0, BLK)
        act[rows, HL:D] = (outA[rows, 0:HL] * 0.125).astype(BF)
        dh[rows, 0:HL] = outA[rows, HL:D].astype(BF)

    def dn1_rows(r0):
        rows = pl.ds(r0, BLK)
        return nt(act[rows, 0:HL], wqkv[0]) + nt(act[rows, HL:D], wqkv[1]) + nt(dh[rows, 0:HL], wqkv[2])

    att_back(t, False)

    flush(ccp)
    flush([yb, xb])
    for q in (zc, xc, yc):
        flush(q.values())
    ar = {}

    def gA(s, r0, n):
        if s == 4:
            return Wd.at[0, pl.ds(r0, n), 0:HL]
        return Wu.at[s // 2, pl.ds(r0, n), (s % 2) * HL : (s % 2) * HL + HL]

    cbase = al(c * HL, 128)
    xbase = al(c * HL + x * 192, 64)
    XFIRST = (True, True, True, True, True)

    def blk_z(s, k):
        if XFIRST[s]:
            return al(xbase + zk[k] * 48, 16), 48
        return al(cbase + zk[k] * 96, 32), 96

    def spot_of(s):
        if XFIRST[s]:
            return al(xbase + z * 48, 16)
        return al(cbase + z * 96 + x * 48, 16)

    def ar_core(s):
        ar[(s, 0)] = xchg(gA(s, al((1 - c) * HL, 128), HL), rA.at[s, 0:HL, :], core)

    def ar_x(s):
        if XFIRST[s]:
            ar[(s, "x")] = xchg(gA(s, al(c * HL + (1 - x) * 192, 64), 192), rA.at[s, 384:576, :], xp)
        else:
            ar[(s, "x")] = xchg(gA(s, al(cbase + z * 96 + (1 - x) * 48, 16), 48), rA.at[s, 672:720, :], xp)

    def ar_xadd(s):
        ar[(s, "x")].wait_recv()
        if XFIRST[s]:
            addto(gA(s, xbase, 192), rA.at[s, 384:576, :])
        else:
            addto(gA(s, spot_of(s), 48), rA.at[s, 672:720, :])

    def ar_z1(s):
        o = 576 if XFIRST[s] else 384
        for i, k in ((0, 1), (1, 3)):
            r0, n = blk_z(s, k)
            ar[(s, "z1", i)] = xchg(gA(s, r0, n), rA.at[s, o + i * n : o + i * n + n, :], z1)

    def ar_z1add(s):
        o = 576 if XFIRST[s] else 384
        for i, k in ((0, 0), (1, 2)):
            r0, n = blk_z(s, k)
            ar[(s, "z1", i)].wait_recv()
            addto(gA(s, r0, n), rA.at[s, o + i * n : o + i * n + n, :])

    def ar_z2(s):
        o = 672 if XFIRST[s] else 576
        r0, n = blk_z(s, 2)
        ar[(s, "z2")] = xchg(gA(s, r0, n), rA.at[s, o : o + n, :], z2)

    def ar_z2add(s):
        o = 672 if XFIRST[s] else 576
        r0, n = blk_z(s, 0)
        ar[(s, "z2")].wait_recv()
        addto(gA(s, r0, n), rA.at[s, o : o + n, :])

    def ar_begin(s):
        ar[(s, 0)].wait_recv()
        addto(gA(s, cbase, HL), rA.at[s, 0:HL, :])
        (ar_x if XFIRST[s] else ar_z1)(s)

    def ar_step2(s):
        if XFIRST[s]:
            ar_xadd(s)
            ar_z1(s)
        else:
            ar_z1add(s)
            ar_z2(s)

    def ar_step3(s):
        if XFIRST[s]:
            ar_z1add(s)
            ar_z2(s)
        else:
            ar_z2add(s)
            ar_x(s)

    def ar_fin(s):
        (ar_z2add if XFIRST[s] else ar_xadd)(s)

    def fslot(s, r0, n):
        return fS.at[s, pl.ds(r0, n), :]

    def ag_z2(s):
        r0, n = blk_z(s, 0)
        f = fslot(s, r0, n)
        ar[(s, "g2")] = xchg(f, f, z2)
        ar[(s, "g1")] = xchg(f, f, z1)

    def ag_z1(s):
        ar[(s, "g2")].wait_recv()
        r0, n = blk_z(s, 2)
        f = fslot(s, r0, n)
        ar[(s, "g3")] = xchg(f, f, z1)

    def ag_zend(s):
        ar[(s, "g1")].wait_recv()
        ar[(s, "g3")].wait_recv()

    def ag_x(s):
        f = fslot(s, xbase, 192) if XFIRST[s] else fslot(s, spot_of(s), 48)
        ar[(s, "gx")] = xchg(f, f, xp)

    def ag_begin(s):
        r0 = spot_of(s)
        fslot(s, r0, 48)[...] = gA(s, r0, 48)[...]
        (ag_z2 if XFIRST[s] else ag_x)(s)

    def ag_step2(s):
        if XFIRST[s]:
            ag_z1(s)
        else:
            ar[(s, "gx")].wait_recv()
            ag_z2(s)

    def ag_step3(s):
        if XFIRST[s]:
            ag_zend(s)
            ag_x(s)
        else:
            ag_z1(s)

    def ag_core(s):
        if XFIRST[s]:
            ar[(s, "gx")].wait_recv()
        else:
            ag_zend(s)
        f = fslot(s, cbase, HL)
        ar[(s, "gc")] = xchg(f, fA.at[s, pl.ds(cbase, HL), :], core)
        load(f, fA.at[s, pl.ds(cbase, HL), :])

    for s, tt in ((3, t), (4, 1 - t)):
        gp = tn(attF[tt], n2[0:H, :])
        gA(s, 0, HL)[...] = gp[:, 0:HL].astype(BF)
        gA(s, HL, HL)[...] = gp[:, HL:D].astype(BF)
        ar_core(s)
    rs_z3((0, 0, 0))
    cda[0].wait_recv()
    att_back(1 - t, True)
    rs_z2((1, 0, 0))
    rs_z1(1, 1)
    cda[1].wait_recv()
    att_back(1 - t, False)

    flush([cO])
    cdn = []
    for o in (1 - t, t):
        r0 = al(oth + o * BLK, BLK)
        finish_rows(r0)
        rows = pl.ds(al(H + o * BLK, BLK), BLK)
        n2[rows, :] = dn1_rows(r0).astype(BF)
        cdn.append(xchg(n2.at[rows, :], rN.at[pl.ds(al(o * BLK, BLK), BLK), :], yp))
    for s in (3, 4):
        ar_begin(s)
    rs_z3((1, 0, 0))
    rs_z2((1, 1, 0))
    att_back(t, True)
    rs_z1(0, 1)
    for b in range(2):
        finish_rows(al(own + b * BLK, BLK))

    def gw(s, src):
        def body(m, carry):
            rows = pl.ds(al(m * BLK, BLK), BLK)
            gA(s, al(m * BLK, BLK), BLK)[...] = nn(nT[rows, :], src[...]).astype(BF)
            return carry

        lax.fori_loop(0, 3, body, 0)
        ar_core(s)

    gw(0, act.at[:, 0:HL])
    gw(1, act.at[:, HL:D])
    ar_begin(0)
    gw(2, dh.at[:, 0:HL])
    ar_begin(1)
    ar_begin(2)
    rs_z3((1, 1, 0))
    rs_xlast()

    vecA[0] = jnp.zeros((16, D), F32)
    for i, row in ((3, sp), (4, s2g), (5, s2b), (6, sd)):
        vecA[0, i : i + 1, :] = row
    vecA[0, pl.ds(8 + 2 * tr[0] + c, 1), :] = bsums[0]
    vecA[0, pl.ds(8 + 2 * tr[1] + c, 1), :] = bsums[1]
    vecA[0, pl.ds(12 + t, 1), 0:HL] = rowsum(act[:, 0:HL].astype(F32))
    vecA[0, pl.ds(12 + t, 1), HL:D] = rowsum(dh[:, 0:HL].astype(F32))
    stok, s1g, s1b = zrow, zrow, zrow
    cgin = []
    for i, o in enumerate((t, 1 - t)):
        o0 = al(o * BLK, BLK)
        r0 = al(own + o0, BLK)
        rows = pl.ds(r0, BLK)
        orow = pl.ds(o0, BLK)
        cdn[i].wait_recv()
        dnb = dn1_rows(r0) + rN[orow, :].astype(F32)
        m, v = start_rows(r0)
        cent, r = stats(v)
        xhat = cent * r
        dst = mid[orow, :] + norm_back(xhat, r, dnb, ln1g)
        ginS[orow, :] = jnp.where(m, 0.0, dst).astype(BF)
        stok = stok + rowsum(jnp.where(m, dst, 0.0))
        s1g = s1g + rowsum(dnb * xhat)
        s1b = s1b + rowsum(dnb)
        if i == 1:
            for n, row in ((0, stok), (1, s1g), (2, s1b)):
                vecA[0, n : n + 1, :] = row
            cv = cv0 = xchg(vecA.at[0], vR.at[0], core)
        cgin.append(xchg(ginS.at[orow, :], gin.at[rows, :], yp))
        load(ginS.at[orow, :], gin.at[rows, :])
        if i == 0:
            ar_step2(0)
            rs_z2((0, 1, 0))
            ar_step2(3)
            ar_step2(4)
            ar_step2(1)
            rs_y(1)
            ar_step2(2)
            ar_step3(0)

    def sum_step(i, to):
        cv.wait_recv()
        vecA[i] = vecA[i - 1] + vR[i - 1]
        return xchg(vecA.at[i], vR.at[i], to)

    ar_step3(3)
    ar_step3(4)
    ar_step3(1)
    rs_z3((0, 1, 0))
    ar_fin(0)
    ag_begin(0)
    ar_step3(2)
    ar_fin(3)
    ar_fin(4)
    cgp = xchg(gA(4, spot_of(4), 48), rgp, yp)
    mixed_send(3)
    cv = sum_step(1, xp)
    ar_fin(1)
    ag_begin(1)
    ag_step2(0)
    ar_fin(2)
    ag_begin(2)
    ag_step2(1)
    ag_step3(0)
    cgp.wait_recv()
    addto(gA(3, spot_of(3), 48), rgp)
    ag_begin(3)
    cv = sum_step(2, z1)
    ag_step2(2)
    ag_step3(1)
    rs_y(0)
    ag_core(0)
    ag_step2(3)
    ag_step3(2)
    cv = sum_step(3, z2)
    ag_core(1)
    ag_step3(3)
    rs_c(0)
    rs_c(1)
    flush([cv0])
    cv = sum_step(4, yp)
    ag_core(2)
    ag_core(3)
    rs_end(0)
    rs_end(1)
    cv.wait_recv()
    vecA[0] = vecA[4] + vR[4]
    load(vecA.at[0], vout)
    for s in range(4):
        ar[(s, "gc")].wait_recv()
    for cp in cmix + cgin:
        cp.wait_recv()
    flush([cp for cp, _ in pending])
    for cp in loads[4:]:
        cp.wait()
    assert (len(pending), slots[0], len(loads)) == (SENT, LANDED, LOCAL)


def scratch():
    def v(shape, dt):
        return pltpu.VMEM(shape, dt)

    return [
        v((T, D), BF), v((D, T), BF), v((3, T, HL), BF), v((T, HL), BF), v((2, H, HL), BF), v((2, HL, D), BF),
        v((2, D, D), BF), v((2, D, D), BF), v((H, D), F32), v((T, D), BF), v((T, D), BF), v((D, T), BF),
        v((T, D), F32), v((T, D), F32), v((H, D), BF), v((H, D), BF), v((T, D), BF), v((T, D), BF),
        v((2, 2, 4, 96, D), BF), v((2, 2, 4, 96, D), BF),
        v((2, 2, 9, 96, D), BF), v((2, 96, D), BF), v((2, 96, D), BF), v((2, 96, D), BF),
        v((2, 96, D), F32), v((2, 48, D), F32), v((T, HL), BF), v((48, HL), BF), v((5, 720, HL), BF),
        v((8, T), F32), v((2, 8, D), F32), v((5, 16, D), F32), v((5, 16, D), F32),
        v((T, D), BF), v((3, D, HL), BF), v((T, 128), jnp.int32), v((1, T), jnp.int32), v((8, D), F32),
        v((H, D), BF), v((H, D), BF), v((4, D, HL), BF), v((2, 48, 2 * D), F32),
        pltpu.SemaphoreType.DMA((SENT,)), pltpu.SemaphoreType.DMA((LANDED,)), pltpu.SemaphoreType.DMA((LOCAL,)),
    ]


def finish(mixed, gin, fa, gup, gdn, vs, o_mixed, o_gin, o_tok, o_g1, o_b1, o_qkv, o_bqv, o_proj, o_bp, o_g2, o_b2, o_up,
           o_bup, o_dn, o_bd, gb, gf, fb, ff, pf, mb, ub, vb, rows_1d, r_bup, r_bqv, sem):
    t = lax.axis_index("tensor")
    count = [0]

    def copy(src, dst):
        cp = pltpu.make_async_copy(src, dst, sem.at[count[0]])
        count[0] += 1
        cp.start()
        return cp

    vc = copy(vs, vb)
    fc = [copy(fa.at[s], fb.at[s]) for s in range(4)]
    gc = [copy(gin.at[b * BLK : b * BLK + BLK, :], gb.at[b * BLK : b * BLK + BLK, :]) for b in range(4)]
    through = [(copy(mixed, mb), mb, o_mixed), (copy(gup, ub.at[0]), ub.at[0], o_up), (copy(gdn, ub.at[1]), ub.at[1], o_dn)]
    out = []
    vc.wait()
    for i, o in enumerate((o_tok, o_g1, o_b1, o_bp, o_g2, o_b2, o_bd)):
        rows_1d[i][...] = vb[i : i + 1, :].reshape(D)
        out.append(copy(rows_1d[i], o))
    for i in range(2):
        r_bup[i * D : i * D + D] = vb[pl.ds(8 + 2 * t + i, 1), :].reshape(D)
        r_bqv[i : i + 1, :] = vb[pl.ds(12 + t, 1), i * HL : i * HL + HL]
    out += [copy(r_bup, o_bup), copy(r_bqv, o_bqv)]
    for b in range(4):
        gc[b].wait()
        rows = slice(b * BLK, b * BLK + BLK)
        gf[rows, :] = gb[rows, :].astype(F32)
        out.append(copy(gf.at[rows, :], o_gin.at[rows, :]))
    for cp, here, there in through:
        cp.wait()
        out.append(copy(here, there))
    for s in range(4):
        fc[s].wait()
        if s < 3:
            ff[s] = fb[s].astype(F32)
            out.append(copy(ff.at[s], o_qkv.at[s]))
        else:
            pf[:, 0:HL] = fb[3, 0:HL, :].astype(F32)
            pf[:, HL:D] = fb[3, HL:D, :].astype(F32)
            out.append(copy(pf, o_proj))
    for cp in out:
        cp.wait()


def on_device(
    patches, image_ids, valid, mask_pos, mask_token, ln1_gain, ln1_bias, w_qkv, b_qv, w_proj, b_proj,
    ln2_gain, ln2_bias, w_up, b_up, w_down, b_down, cotangent,
):
    vm = pl.BlockSpec(memory_space=pltpu.VMEM)
    hbm = pl.BlockSpec(memory_space=pl.ANY)
    sds = jax.ShapeDtypeStruct
    parts = pl.pallas_call(
        mega,
        out_shape=(
            sds((T, D), BF), sds((T, D), BF), sds((4, D, HL), BF), sds((48, 2 * D), F32), sds((48, 2 * D), F32),
            sds((16, D), F32),
        ),
        in_specs=[hbm if i in (0, 11, 13, 17) else vm for i in range(18)],
        out_specs=(hbm,) * 6,
        scratch_shapes=scratch(),
        compiler_params=pltpu.CompilerParams(collective_id=0, has_side_effects=True, vmem_limit_bytes=66584576),
        name="block",
    )(
        patches, image_ids, valid, mask_pos, mask_token, ln1_gain, ln1_bias, b_proj, ln2_gain, ln2_bias, b_down,
        jnp.transpose(w_qkv, (1, 0, 2)), b_qv, w_proj, w_up, w_down.T, b_up, cotangent,
    )
    row = sds((D,), F32)
    outs = pl.pallas_call(
        finish,
        out_shape=(
            sds((T, D), BF), sds((T, D), F32), row, row, row, sds((3, D, HL), F32), sds((2, HL), F32), sds((HL, D), F32),
            row, row, row, sds((48, 2 * D), F32), sds((2 * D,), F32), sds((48, 2 * D), F32), row,
        ),
        in_specs=[hbm] * 6,
        out_specs=(hbm,) * 15,
        scratch_shapes=[
            pltpu.VMEM((T, D), BF), pltpu.VMEM((T, D), F32), pltpu.VMEM((4, D, HL), BF), pltpu.VMEM((3, D, HL), F32),
            pltpu.VMEM((HL, D), F32), pltpu.VMEM((T, D), BF), pltpu.VMEM((2, 48, 2 * D), F32),
            pltpu.VMEM((16, D), F32), [pltpu.VMEM((D,), F32)] * 7, pltpu.VMEM((2 * D,), F32), pltpu.VMEM((2, HL), F32),
            pltpu.SemaphoreType.DMA((32,)),
        ],
        compiler_params=pltpu.CompilerParams(vmem_limit_bytes=66584576),
        name="finish",
    )(*parts)
    outs = list(outs)
    outs[5] = jnp.transpose(outs[5], (1, 0, 2))
    outs[13] = outs[13].T
    return tuple(outs)


HEAD_DIM = 64


def norm_rows(values, gain, shift):
    mean = jnp.mean(values, axis=-1, keepdims=True)
    cent = values - mean
    var = jnp.mean(cent * cent, axis=-1, keepdims=True)
    return cent * lax.rsqrt(var + EPS) * gain + shift


def left_dot(first, second):
    return lax.dot_general(
        first, second, (((0,), (0,)), ((), ())), preferred_element_type=jnp.float32
    )


def right_dot(first, second):
    return lax.dot_general(
        first, second, (((1,), (1,)), ((), ())), preferred_element_type=jnp.float32
    )


def allowed_rows(ids, live, begin, count):
    rows = ids.shape[0]
    own_ids = lax.dynamic_slice_in_dim(ids, begin, count, 0)
    places = begin + jnp.arange(count)
    same_place = places[:, None] == jnp.arange(rows)[None, :]
    return (own_ids[:, None] == ids[None, :]) & ((live[None, :] == 1) | same_place)


def spread(
    patches,
    image_ids,
    valid,
    mask_pos,
    mask_token,
    ln1_gain,
    ln1_bias,
    w_qkv,
    b_qv,
    w_proj,
    b_proj,
    ln2_gain,
    ln2_bias,
    w_up,
    b_up,
    w_down,
    b_down,
    cotangent,
):
    rows = patches.shape[0]
    local_width = w_qkv.shape[2]
    local_heads = local_width // HEAD_DIM
    scale = 1.0 / HEAD_DIM**0.5
    ids = image_ids[0]
    live = valid[0]
    masked = mask_pos[0][:, None] == 1
    block = min(512, rows)
    blocks = rows // block
    start = jnp.where(masked, mask_token.astype(jnp.float32)[None, :], patches.astype(jnp.float32))
    normed, norm1_pull = jax.vjp(
        norm_rows, start, ln1_gain.astype(jnp.float32), ln1_bias.astype(jnp.float32)
    )
    normed_b = normed.astype(jnp.bfloat16)
    qv_bias = b_qv.astype(jnp.float32)
    bias = jnp.stack([qv_bias[0], jnp.zeros_like(qv_bias[0]), qv_bias[1]])
    qkv = jnp.einsum("td,dsc->tsc", normed_b, w_qkv, preferred_element_type=jnp.float32)
    qkv_b = (qkv + bias[None]).astype(jnp.bfloat16)
    query = qkv_b[:, 0].reshape(rows, local_heads, HEAD_DIM)
    keys = qkv_b[:, 1].reshape(rows, local_heads, HEAD_DIM)
    values = qkv_b[:, 2].reshape(rows, local_heads, HEAD_DIM)
    outputs = []
    totals = []
    for index in range(blocks):
        begin = index * block
        query_part = query[begin : begin + block]
        allowed = allowed_rows(ids, live, begin, block)
        scores = (
            jnp.einsum("qhc,khc->hqk", query_part, keys, preferred_element_type=jnp.float32) * scale
        )
        scores = jnp.where(allowed[None], scores, -1e30)
        top = jnp.max(scores, axis=-1, keepdims=True)
        expd = jnp.exp(scores - top)
        summed = jnp.sum(expd, axis=-1, keepdims=True)
        probs_b = (expd / summed).astype(jnp.bfloat16)
        totals.append(top + jnp.log(summed))
        outputs.append(
            jnp.einsum("hqk,khc->qhc", probs_b, values, preferred_element_type=jnp.float32)
        )
    attended_b = jnp.concatenate(outputs, axis=0).reshape(rows, local_width).astype(jnp.bfloat16)
    attn_part = jnp.dot(attended_b, w_proj, preferred_element_type=jnp.float32)
    ln2_gain_f = ln2_gain.astype(jnp.float32)
    ln2_bias_f = ln2_bias.astype(jnp.float32)
    attn_total = lax.psum(attn_part, "tensor")
    middle = start + attn_total + b_proj.astype(jnp.float32)
    normed2, norm2_pull = jax.vjp(norm_rows, middle, ln2_gain_f, ln2_bias_f)
    normed2_b = normed2.astype(jnp.bfloat16)
    up_full, down_full = (
        lax.all_gather(w_up, "dp", axis=0, tiled=True),
        lax.all_gather(w_down, "dp", axis=1, tiled=True),
    )
    hidden = jnp.dot(normed2_b, up_full, preferred_element_type=jnp.float32) + b_up.astype(
        jnp.float32
    )
    active, gelu_pull = jax.vjp(partial(jax.nn.gelu, approximate=False), hidden)
    active_b = active.astype(jnp.bfloat16)
    mlp_part = jnp.dot(active_b, down_full, preferred_element_type=jnp.float32)
    mlp_total = lax.psum(mlp_part.astype(jnp.bfloat16), "tensor").astype(jnp.float32)
    mixed = (middle + mlp_total + b_down.astype(jnp.float32)).astype(jnp.bfloat16)
    seed_grad = cotangent.astype(jnp.float32)
    up_back, down_back = (up_full, down_full)
    grad_b_down = jnp.sum(seed_grad, axis=0)
    grad_down_local = left_dot(active_b, cotangent)
    grad_active = right_dot(cotangent, down_back)
    (grad_hidden,) = gelu_pull(grad_active)
    grad_hidden_b = grad_hidden.astype(jnp.bfloat16)
    grad_b_up = jnp.sum(grad_hidden_b.astype(jnp.float32), axis=0)
    grad_up_local = left_dot(normed2_b, grad_hidden_b)
    grad_normed2_part = right_dot(grad_hidden_b, up_back)
    grad_normed2 = lax.psum(grad_normed2_part, "tensor")
    grad_mid_norm, grad_ln2_gain, grad_ln2_bias = norm2_pull(grad_normed2)
    grad_middle = seed_grad + grad_mid_norm
    grad_w_up, grad_w_down = (
        lax.psum_scatter(grad_up_local, "dp", scatter_dimension=0, tiled=True),
        lax.psum_scatter(grad_down_local, "dp", scatter_dimension=1, tiled=True),
    )
    grad_branch_b = grad_middle.astype(jnp.bfloat16)
    grad_b_proj = jnp.sum(grad_branch_b.astype(jnp.float32), axis=0)
    grad_w_proj = left_dot(attended_b, grad_branch_b)
    grad_attended = (
        right_dot(grad_branch_b, w_proj).astype(jnp.bfloat16).reshape(rows, local_heads, HEAD_DIM)
    )
    grad_query_parts = []
    grad_keys = jnp.zeros((rows, local_heads, HEAD_DIM), jnp.float32)
    grad_values = jnp.zeros((rows, local_heads, HEAD_DIM), jnp.float32)
    for index in range(blocks):
        begin = index * block
        query_part = query[begin : begin + block]
        grad_out_part = grad_attended[begin : begin + block]
        allowed = allowed_rows(ids, live, begin, block)
        scores = (
            jnp.einsum("qhc,khc->hqk", query_part, keys, preferred_element_type=jnp.float32) * scale
        )
        scores = jnp.where(allowed[None], scores, -1e30)
        probs = jnp.exp(scores - totals[index])
        probs_b = probs.astype(jnp.bfloat16)
        grad_values = grad_values + jnp.einsum(
            "hqk,qhc->khc", probs_b, grad_out_part, preferred_element_type=jnp.float32
        )
        grad_probs = jnp.einsum(
            "qhc,khc->hqk", grad_out_part, values, preferred_element_type=jnp.float32
        )
        inner = jnp.sum(probs * grad_probs, axis=-1, keepdims=True)
        grad_scores_b = (probs * (grad_probs - inner)).astype(jnp.bfloat16)
        grad_query_parts.append(
            jnp.einsum("hqk,khc->qhc", grad_scores_b, keys, preferred_element_type=jnp.float32)
            * scale
        )
        grad_keys = (
            grad_keys
            + jnp.einsum(
                "hqk,qhc->khc", grad_scores_b, query_part, preferred_element_type=jnp.float32
            )
            * scale
        )
    grad_query = jnp.concatenate(grad_query_parts, axis=0)
    grad_qkv_b = (
        jnp.stack([grad_query, grad_keys, grad_values], axis=1)
        .reshape(rows, 3, local_width)
        .astype(jnp.bfloat16)
    )
    grad_qkv_f = grad_qkv_b.astype(jnp.float32)
    grad_b_qv = jnp.stack([jnp.sum(grad_qkv_f[:, 0], axis=0), jnp.sum(grad_qkv_f[:, 2], axis=0)])
    grad_w_qkv = jnp.einsum("td,tsc->dsc", normed_b, grad_qkv_b, preferred_element_type=jnp.float32)
    grad_normed_part = jnp.einsum(
        "tsc,dsc->td", grad_qkv_b, w_qkv, preferred_element_type=jnp.float32
    )
    grad_normed = lax.psum(grad_normed_part.astype(jnp.bfloat16), "tensor").astype(jnp.float32)
    grad_start_norm, grad_ln1_gain, grad_ln1_bias = norm1_pull(grad_normed)
    grad_start = grad_middle + grad_start_norm
    grad_input = jnp.where(masked, 0.0, grad_start)
    grad_token = jnp.sum(jnp.where(masked, grad_start, 0.0), axis=0)
    summed = lax.psum(
        (
            grad_token,
            grad_ln1_gain,
            grad_ln1_bias,
            grad_w_qkv,
            grad_b_qv,
            grad_w_proj,
            grad_b_proj,
            grad_ln2_gain,
            grad_ln2_bias,
            grad_b_up,
            grad_b_down,
        ),
        "dp",
    )
    return (
        mixed,
        grad_input,
        summed[0],
        summed[1],
        summed[2],
        summed[3],
        summed[4],
        summed[5],
        summed[6],
        summed[7],
        summed[8],
        grad_w_up,
        summed[9],
        grad_w_down,
        summed[10],
    )


def solution(mesh):
    placed = (
        P("dp", None),
        P("dp", None),
        P("dp", None),
        P("dp", None),
        P(),
        P(),
        P(),
        P(None, None, "tensor"),
        P(None, "tensor"),
        P("tensor", None),
        P(),
        P(),
        P(),
        P("dp", "tensor"),
        P("tensor"),
        P("tensor", "dp"),
        P(),
        P("dp", None),
    )
    fits = mesh.shape["dp"] == 16 and mesh.shape["tensor"] == 2
    return jax.shard_map(
        on_device if fits else spread,
        mesh=mesh,
        in_specs=placed,
        out_specs=(
            P("dp", None),
            P("dp", None),
            P(),
            P(),
            P(),
            P(None, None, "tensor"),
            P(None, "tensor"),
            P("tensor", None),
            P(),
            P(),
            P(),
            P("dp", "tensor"),
            P("tensor"),
            P("tensor", "dp"),
            P(),
        ),
        check_vma=False,
    )
```

profile of v0, /device:TPU:0, one launch (start us, length us, event | category | flops | bytes accessed | tf_op | source)
XLA Modules:
  0.0 147.2 jit_solution(13524749105217212759)
XLA Ops:
  0.7 140.4 %block.1 = (bf16[1024,768]{1,0:T(8,128)(2,1)}, bf16[1024,768]{1,0:T(8,128)(2,1)}, bf16[4,768,384]{2,1,0:T(8,128)(2,1)}, f32[48,1536]{1,0:T(8,128)}, f32[48,1536]{1,0:T(8,128)}, /*index=5*/f32[16,768]{1,0:T(8,128)}) custom-call(bf16[1024,768]{1,0:T(8,128)(2,1)} %patches.1, s32[1,1024]{1,0:T(1,128)} %ids.1, s32[1,1024]{1,0:T(1,128)} %live.1, ...), custom_call_target="tpu_custom_call" | custom-call | tf_op jit(solution)/shard_map/block/pallas_call | solution.py:999
  141.1 5.9 %finish.1 = (bf16[1024,768]{1,0:T(8,128)(2,1)}, f32[1024,768]{1,0:T(8,128)}, f32[768]{0:T(1024)}, f32[768]{0:T(1024)}, f32[768]{0:T(1024)}, /*index=5*/f32[3,768...) custom-call(bf16[1024,768]{1,0:T(8,128)(2,1)} %get-tuple-element.36., ...), custom_call_target="tpu_custom_call" | custom-call | tf_op jit(solution)/shard_map/finish/pallas_call | solution.py:1015
where the time goes:
time: 147 us
  Pallas kernels  146 us (99%)
    pallas_call x1, Pallas kernels, on_device(): pl.pallas_call(mega, out_shape=(sds((T, D), BF), sds((T, D), BF), sds((4,...  140 us
    pallas_call x1, Pallas kernels, on_device(): pl.pallas_call(finish, out_shape=(sds((T, D), BF), sds((T, D), F32), row,...  5.9 us

commit v1 on v0

--- a/solution.py
+++ b/solution.py
@@ -18,7 +18,7 @@
 BLK = 256
 WIN = 768
 CUT = 640
-SENT, LANDED, LOCAL = 148, 143, 17
+SENT, LANDED, LOCAL = 145, 140, 31
 
 
 def nn(a, b):
@@ -56,12 +56,12 @@
 
 
 def mega(
-    patches, ids, live, hidden_pos, token_b, ln1g_b, ln1b_b, bproj_b, ln2g_b, ln2b_b, bdown_b, wqkv_h, bqv_b, wproj,
-    up, dn, bup, cot,
+    patches, wqkv_h, wproj, cot, ids_h, live_h, hidden_h, token_h, ln1g_h, ln1b_h, bproj_h, ln2g_h, ln2b_h, bdown_h, bqv_h,
+    up_h, dn_h, bup_h,
     mixed, gin, fA, gup, gdn, vout,
     n1, nT, qkv, attO, attF, wpf, Wu, Wd, mid, n2, dml, dmlT, outA, dn2A, rO, rN, act, dh, gU, gD,
     rG, rX, sy, ry, sc, rc, dO, rgp, rA, lseT, bupA, vecA, vR, pat, wqkv, codec, coder, vec, mixS, ginS, fS,
-    gS, ssem, rsem, lsem,
+    gS, small, ssem, rsem, lsem,
 ):
     d = lax.axis_index("dp")
     t = lax.axis_index("tensor")
@@ -135,8 +135,15 @@
         loads.append(cp)
         return cp
 
+    ids, live, hidden_pos, token_b, ln1g_b, ln1b_b, bproj_b, ln2g_b, ln2b_b, bdown_b, bqv_b, up, dn, bup = small
+    sources = (
+        ids_h, live_h, hidden_h, token_h, ln1g_h, ln1b_h, bproj_h, ln2g_h, ln2b_h, bdown_h, bqv_h, up_h, dn_h, bup_h
+    )
+    first = [load(src, dst) for src, dst in zip(sources, small)]
     lpat = load(patches, pat)
     lwq = load(wqkv_h, wqkv)
+    for cp in first:
+        cp.wait()
     code = ids[...] + 16 * live[...] + 32 * hidden_pos[...]
     coder[...] = code
     codec[...] = jnp.broadcast_to(code.astype(F32), (128, T)).T.astype(jnp.int32)
@@ -356,7 +363,7 @@
         dst[...] = (dst[...].astype(F32) + src[...].astype(F32)).astype(BF)
 
     def rs_x(a, j):
-        rs[(a, j)] = [xchg(G[a].at[j, 1, h * 2 : h * 2 + 2], rG.at[a, j, h * 2 : h * 2 + 2], xp) for h in (0, 1)]
+        rs[(a, j)] = [xchg(G[a].at[j, 1], rG.at[a, j, 0:4], xp)]
 
     rland = {(r, q): slot() for r in ((0, 0, 0), (0, 0, 1), (0, 1, 0), (1, 0, 0), (1, 1, 0)) for q in range(4, 9)}
 
@@ -585,6 +592,10 @@
     rs_z2((0, 0, 0))
     outA[...] = jnp.zeros((T, D), F32)
     nT[...] = n1[...].T
+    flush(ccp)
+    flush([yb, xb])
+    for q in (zc, xc, yc):
+        flush(q.values())
     rs_z1(1, 0)
 
     def att_back(half, edge):
@@ -640,10 +651,6 @@
 
     att_back(t, False)
 
-    flush(ccp)
-    flush([yb, xb])
-    for q in (zc, xc, yc):
-        flush(q.values())
     ar = {}
 
     def gA(s, r0, n):
@@ -819,6 +826,7 @@
         lax.fori_loop(0, 3, body, 0)
         ar_core(s)
 
+    before = [cp for cp, _ in pending]
     gw(0, act.at[:, 0:HL])
     gw(1, act.at[:, HL:D])
     ar_begin(0)
@@ -899,6 +907,7 @@
     ag_step2(2)
     ag_step3(1)
     rs_y(0)
+    flush(before[:-12])
     ag_core(0)
     ag_step2(3)
     ag_step3(2)
@@ -909,6 +918,8 @@
     rs_c(1)
     flush([cv0])
     cv = sum_step(4, yp)
+    flush(before)
+    flush([ar[k] if not isinstance(ar[k], list) else ar[k][0] for k in ar if k[1] in (0, "x", "z1", "z2")])
     ag_core(2)
     ag_core(3)
     rs_end(0)
@@ -921,7 +932,7 @@
     for cp in cmix + cgin:
         cp.wait_recv()
     flush([cp for cp, _ in pending])
-    for cp in loads[4:]:
+    for cp in loads[18:]:
         cp.wait()
     assert (len(pending), slots[0], len(loads)) == (SENT, LANDED, LOCAL)
 
@@ -940,6 +951,7 @@
         v((8, T), F32), v((2, 8, D), F32), v((5, 16, D), F32), v((5, 16, D), F32),
         v((T, D), BF), v((3, D, HL), BF), v((T, 128), jnp.int32), v((1, T), jnp.int32), v((8, D), F32),
         v((H, D), BF), v((H, D), BF), v((4, D, HL), BF), v((2, 48, 2 * D), F32),
+        [v((1, T), jnp.int32)] * 3 + [v((D,), BF)] * 7 + [v((2, HL), BF)] + [v((48, 2 * D), BF)] * 2 + [v((2 * D,), BF)],
         pltpu.SemaphoreType.DMA((SENT,)), pltpu.SemaphoreType.DMA((LANDED,)), pltpu.SemaphoreType.DMA((LOCAL,)),
     ]
 
@@ -993,7 +1005,6 @@
     patches, image_ids, valid, mask_pos, mask_token, ln1_gain, ln1_bias, w_qkv, b_qv, w_proj, b_proj,
     ln2_gain, ln2_bias, w_up, b_up, w_down, b_down, cotangent,
 ):
-    vm = pl.BlockSpec(memory_space=pltpu.VMEM)
     hbm = pl.BlockSpec(memory_space=pl.ANY)
     sds = jax.ShapeDtypeStruct
     parts = pl.pallas_call(
@@ -1002,14 +1013,14 @@
             sds((T, D), BF), sds((T, D), BF), sds((4, D, HL), BF), sds((48, 2 * D), F32), sds((48, 2 * D), F32),
             sds((16, D), F32),
         ),
-        in_specs=[hbm if i in (0, 11, 13, 17) else vm for i in range(18)],
+        in_specs=[hbm] * 18,
         out_specs=(hbm,) * 6,
         scratch_shapes=scratch(),
         compiler_params=pltpu.CompilerParams(collective_id=0, has_side_effects=True, vmem_limit_bytes=66584576),
         name="block",
     )(
-        patches, image_ids, valid, mask_pos, mask_token, ln1_gain, ln1_bias, b_proj, ln2_gain, ln2_bias, b_down,
-        jnp.transpose(w_qkv, (1, 0, 2)), b_qv, w_proj, w_up, w_down.T, b_up, cotangent,
+        patches, jnp.transpose(w_qkv, (1, 0, 2)), w_proj, cotangent, image_ids, valid, mask_pos, mask_token, ln1_gain,
+        ln1_bias, b_proj, ln2_gain, ln2_bias, b_down, b_qv, w_up, w_down.T, b_up,
     )
     row = sds((D,), F32)
     outs = pl.pallas_call(

time: 147 us -> 146 us (level)
  no operation moved by 1% of the time
where the time goes in v1:
time: 146 us
  Pallas kernels  145 us (99%)
    pallas_call x1, Pallas kernels, on_device(): pl.pallas_call(mega, out_shape=(sds((T, D), BF), sds((T, D), BF), sds((4,...  139 us
    pallas_call x1, Pallas kernels, on_device(): pl.pallas_call(finish, out_shape=(sds((T, D), BF), sds((T, D), F32), row,...  5.9 us

profile of v1, /device:TPU:0, one launch (start us, length us, event | category | flops | bytes accessed | tf_op | source)
XLA Modules:
  0.0 146.1 jit_solution(7744411908264136977)
XLA Ops:
  0.7 139.3 %block.1 = (bf16[1024,768]{1,0:T(8,128)(2,1)}, bf16[1024,768]{1,0:T(8,128)(2,1)}, bf16[4,768,384]{2,1,0:T(8,128)(2,1)}, f32[48,1536]{1,0:T(8,128)}, f32[48,1536]{1,0:T(8,128)}, /*index=5*/f32[16,768]{1,0:T(8,128)}) custom-call(bf16[1024,768]{1,0:T(8,128)(2,1)} %patches.1, bf16[3,768,384]{2,1,0:T(8,128)(2,1)} %bitcast.4, bf16[384,768]{1,0:T(8,128)(2,1)} %wproj.1, ...), custom_call_target="tpu_custom_call" | custom-call | tf_op jit(solution)/shard_map/block/pallas_call | solution.py:1010
  140.0 5.9 %finish.1 = (bf16[1024,768]{1,0:T(8,128)(2,1)}, f32[1024,768]{1,0:T(8,128)}, f32[768]{0:T(1024)}, f32[768]{0:T(1024)}, f32[768]{0:T(1024)}, /*index=5*/f32[3,768...) custom-call(bf16[1024,768]{1,0:T(8,128)(2,1)} %get-tuple-element.36., ...), custom_call_target="tpu_custom_call" | custom-call | tf_op jit(solution)/shard_map/finish/pallas_call | solution.py:1026
